TPU v7x, 1024 devices: a whole 8x8x8 slice. The times are simulated.
1024 devices in a mesh: section: 8 (over y), expert: 16 (over x, core), tensor: 8 (over z).
Axes of the slice: x: 8, y: 8, z: 8, core: 2. Of those that a mesh axis runs over, the one named last changes fastest.
Arguments:
- tokens: bfloat16 [16384, 4096], P(('section', 'expert'), 'tensor'), may hold values from -6 to 6
- w_gate: bfloat16 [8, 16, 4096, 1536], P('section', 'expert', None, 'tensor'), may hold values from -0.09375 to 0.09375
- w_up: bfloat16 [8, 16, 4096, 1536], P('section', 'expert', None, 'tensor'), may hold values from -0.09375 to 0.09375
- hidden_grad: bfloat16 [8, 16, 256, 1536], P('section', 'expert', None, 'tensor'), may hold values from -6 to 6
- routes: int32 [16384, 8], P(('section', 'expert')), may hold values from 0 to 127, as said below
- slots: int32 [16384, 8], P(('section', 'expert')), may hold values from 0 to 16, as said below
- pad_mask: int32 [16384], P(('section', 'expert')), may hold values 0 or 1
Outputs:
- upstream: bfloat16 [16384, 4096], P(('section', 'expert'), 'tensor')
Inputs may be any that keep to these rules, and one draw needn't show every extreme that they name: `routes`: each row names 8 different experts. In every section one expert e with e mod 8 = 0 is named by 16 or more rows of every block of 128 rows. `slots`: within each block of 128 rows (the rows of one device), the routes naming one expert, taken in order of row and then of position in the row, hold 0, 1, 2 and so on; those from the 16-th on hold 16.
All inputs are finite; a program needn't handle non-finite values. No bound on the sum of `pad_mask` on one device may be relied on, other than what follows from the above.
Results may differ from a plain program's by a relative error of at most 0.018.
Values may be sent and summed in bfloat16 or wider, within the bound.
A program may use at most 32 MiB of HBM per device.

v0:
```python
import jax
import jax.numpy as jnp
from jax import lax
from jax.sharding import PartitionSpec as P

EXP_DEV = 8


def passed_along(value, axis, steps):
    count = lax.axis_size(axis)
    first, last = (max(0, -steps), min(count, count - steps))
    return lax.ppermute(value, axis, [(source, source + steps) for source in range(first, last)])


def slot_tables(routes, slots, pad_mask, total_rows, capacity):
    live = (routes % EXP_DEV == 0) & (slots < capacity)
    target = jnp.where(live, routes // EXP_DEV * capacity + slots, -1)
    positions = lax.broadcasted_iota(jnp.int32, (total_rows, routes.shape[0]), 0)
    hits = jnp.zeros((total_rows, routes.shape[0]), jnp.float32)
    for k in range(routes.shape[1]):
        hits = hits + (positions == target[:, k][None, :]).astype(jnp.float32)
    keep = hits * pad_mask[None, :].astype(jnp.float32)
    return (hits.astype(jnp.bfloat16), keep)


def shards(tokens, w_gate, w_up, hidden_grad, routes, slots, pad_mask):
    count = lax.axis_size("expert")
    total_rows = hidden_grad.shape[2]
    capacity = total_rows // count
    pick, keep = slot_tables(routes, slots, pad_mask, total_rows, capacity)
    gate_w = w_gate[0, 0]
    up_w = w_up[0, 0]
    grad_a = hidden_grad[0, 0]
    contract_last = (((1,), (1,)), ((), ()))
    contract_first = (((0,), (0,)), ((), ()))
    whole = lax.all_gather(tokens, "tensor", axis=1, tiled=True)
    sent = jnp.dot(pick, whole, preferred_element_type=jnp.float32).astype(jnp.bfloat16)
    arrived = lax.all_to_all(sent, "expert", split_axis=0, concat_axis=0, tiled=True)
    pre_gate = jnp.dot(arrived, gate_w, preferred_element_type=jnp.float32)
    pre_up = jnp.dot(arrived, up_w, preferred_element_type=jnp.float32)
    sig = jax.nn.sigmoid(pre_gate)
    act = grad_a.astype(jnp.float32)
    up_grad = (act * pre_gate * sig).astype(jnp.bfloat16)
    gate_grad = (act * pre_up * sig * (1.0 + pre_gate * (1.0 - sig))).astype(jnp.bfloat16)
    partial_value = lax.dot_general(
        gate_grad, gate_w, contract_last, preferred_element_type=jnp.float32
    )
    partial_value = partial_value + lax.dot_general(
        up_grad, up_w, contract_last, preferred_element_type=jnp.float32
    )
    back = lax.all_to_all(
        partial_value.astype(jnp.bfloat16), "expert", split_axis=0, concat_axis=0, tiled=True
    )
    summed = lax.dot_general(
        keep.astype(jnp.bfloat16), back, contract_first, preferred_element_type=jnp.float32
    )
    grads = lax.psum_scatter(summed.astype(jnp.bfloat16), "tensor", scatter_dimension=1, tiled=True)
    return passed_along(grads, "section", -1)


def solution(mesh):
    placed = (
        P(("section", "expert"), "tensor"),
        P("section", "expert", None, "tensor"),
        P("section", "expert", None, "tensor"),
        P("section", "expert", None, "tensor"),
        P(("section", "expert"), None),
        P(("section", "expert"), None),
        P(("section", "expert")),
    )
    return jax.shard_map(
        shards,
        mesh=mesh,
        in_specs=placed,
        out_specs=P(("section", "expert"), "tensor"),
        check_vma=False,
    )
```

profile of v0, /device:TPU:52, one launch (start us, length us, event | category | flops | bytes accessed | tf_op | source)
XLA Modules:
  0.0 252.0 jit_solution(4713082257712101882)
XLA Ops:
  6.5 0.0 copy-start
  6.5 0.0 all-gather.2.cloned.1.call-start
  6.5 0.7 all-gather.2.cloned.1.call-update
  7.3 0.7 fusion.55
  8.0 58.6 %all-gather.2.cloned.1.call-done = bf16[128,4096]{1,0:T(8,128)(2,1)} async-done(((bf16[128,512]{1,0:T(8,128)(2,1)}), bf16[128,4096]{1,0:T(8,128)(2,1)}) %all-gather.2.cloned.1.call-update) | async-done | bytes 1048592 | tf_op jit(solution)/shard_map/all_gather | solution.py:36
  66.6 2.0 convolution_convert_fusion
  68.6 0.0 copy-start.2
  68.6 55.8 %all_to_all.24 = bf16[16,16,4096]{2,1,0:T(8,128)(2,1)S(1)} all-to-all(bf16[16,16,4096]{2,1,0:T(8,128)(2,1)S(1)} %bitcast.56), channel_id=1, replica_groups=mesh['section'=8,'expert'=16,'tensor'=8] {'expert'}, dimensions={0} | all-to-all | bytes 4194304 | tf_op jit(solution)/shard_map/all_to_all | solution.py:38
  124.4 0.0 copy-start.1
  124.4 0.0 copy-start.3
  124.4 1.3 copy-done.1
  125.7 0.0 copy-done.2
  125.7 0.8 fusion.3
  126.6 0.0 copy-done
  126.6 0.0 copy-done.3
  126.6 6.1 %fusion.1 = f32[256,4096]{1,0:T(8,128)} fusion(bf16[1,1,4096,192]{2,3,1,0:T(8,128)(2,1)S(1)} %copy-done.2, bf16[256,4096]{1,0:T(8,128)(2,1)} %bitcast.55, bf16[1,1,4096,192]{2,3,1,0:T(8,128)(2,1)S(1)} %copy-done, f32[256,192]{0,1:T(8,128)S(1)} %fusion.3, bf16[1,1,256,192]{2,3,1,0:T(8,128)(2,1)S(1)} %copy-done.3), kind=kOutput, calls=%fused_computation.4 | convolution fusion | flops 805847040 | bytes 9732096 | tf_op jit(solution)/shard_map/dot_general | solution.py:45
  132.7 4.3 %fusion = bf16[256,4096]{1,0:T(8,128)(2,1)} fusion(f32[256,4096]{1,0:T(8,128)} %fusion.1, bf16[1,1,4096,192]{2,3,1,0:T(8,128)(2,1)S(1)} %copy-done, f32[256,192]{0,1:T(8,128)S(1)} %fusion.3, bf16[1,1,256,192]{2,3,1,0:T(8,128)(2,1)S(1)} %copy-done.3), kind=kOutput, calls=%fused_computation.2 | convolution fusion | flops 405094400 | bytes 8159232 | tf_op jit(solution)/shard_map/dot_general | solution.py:48
  137.0 0.0 copy-start.4
  137.0 5.5 %all-to-all-start.1 = ((bf16[16,16,4096]{2,1,0:T(8,128)(2,1)}), bf16[16,16,4096]{2,1,0:T(8,128)(2,1)}, u32[]{:S(2)}, u32[]{:S(2)}) async-start(bf16[16,16,4096]{2,1,0:T(8,128)(2,1)} %bitcast.57), calls=%async_computation.1 | async-start | bytes 4194304 | tf_op jit(solution)/shard_map/all_to_all | solution.py:51
  142.4 0.0 reduce-scatter.2.cloned.1.call-start
  142.5 0.0 copy-done.4
  142.5 47.5 %all-to-all-done.1 = bf16[16,16,4096]{2,1,0:T(8,128)(2,1)} async-done(((bf16[16,16,4096]{2,1,0:T(8,128)(2,1)}), bf16[16,16,4096]{2,1,0:T(8,128)(2,1)}, u32[]{:S(2)}, u32[]{:S(2)}) %all-to-all-start.1) | async-done | bytes 2097184 | tf_op jit(solution)/shard_map/all_to_all | solution.py:51
  190.0 3.1 %convolution_convert_fusion.1 = bf16[128,4096]{1,0:T(8,128)(2,1)} fusion(bf16[256,4096]{1,0:T(8,128)(2,1)} %bitcast.15, f32[128]{0:T(128)S(1)} %convert_element_type.63, s32[128]{0:T(128)S(1)} %get-tuple-element.6, s32[128]{0:T(128)S(1)} %get-tuple-element.7, s32[128]{0:T(128)S(1)} %get-tuple-element.8, s32[128]{0:T(128)S(1)} %get-tuple-element.9, ...), kind=kOutput, calls=%fused_computation.3 | convolution fusion | flops 269778944 | bytes 3150336 | tf_op jit(solution)/shard_map/dot_general | solution.py:54
  193.1 0.0 reduce-scatter.2.cloned.1.call-update
  193.1 43.1 %reduce-scatter.2.cloned.1.call-done = bf16[128,512]{1,0:T(8,128)(2,1)} async-done(((bf16[128,4096]{1,0:T(8,128)(2,1)}), bf16[128,512]{1,0:T(8,128)(2,1)}) %reduce-scatter.2.cloned.1.call-update) | async-done | bytes 131088 | tf_op jit(solution)/shard_map/reduce_scatter | solution.py:57
  236.3 2.4 collective-permute-start
  238.7 5.8 %collective-permute-done = bf16[128,512]{1,0:T(8,128)(2,1)S(1)} collective-permute-done((bf16[128,512]{1,0:T(8,128)(2,1)}, bf16[128,512]{1,0:T(8,128)(2,1)S(1)}, u32[]{:S(2)}, u32[]{:S(2)}) %collective-permute-start) | collective-permute-done | bytes 131104 | tf_op jit(solution)/shard_map/ppermute | solution.py:12
  244.5 0.7 copy.9
  (2 shorter events, 0.0 us)
Async XLA Ops:
  6.5 120.1 %copy-start = (bf16[1,1,4096,192]{2,3,1,0:T(8,128)(2,1)S(1)}, bf16[1,1,4096,192]{2,3,1,0:T(8,128)(2,1)}, u32[]{:S(2)}) copy-start(bf16[1,1,4096,192]{2,3,1,0:T(8,128)(2,1)} %param.9) | copy-start | bytes 4718596
  6.5 60.1 %all-gather.2.cloned.1.call-start = ((), (), s32[]{:S(2)}) async-start(), calls=%async_computation.3 | async-start | bytes 1179648 | tf_op jit(solution)/shard_map/all_gather | solution.py:36
  68.6 57.2 %copy-start.2 = (bf16[1,1,4096,192]{2,3,1,0:T(8,128)(2,1)S(1)}, bf16[1,1,4096,192]{2,3,1,0:T(8,128)(2,1)}, u32[]{:S(2)}) copy-start(bf16[1,1,4096,192]{2,3,1,0:T(8,128)(2,1)} %param.8) | copy-start | bytes 4718596
  124.4 1.3 copy-start.1
  124.4 2.2 copy-start.3
  137.0 5.5 %copy-start.4 = (s32[128]{0:T(128)S(1)}, s32[128]{0:T(128)}, u32[]{:S(2)}) copy-start(s32[128]{0:T(128)} %param.13) | copy-start | bytes 1540
  137.0 53.0 %all-to-all-start.1 = ((bf16[16,16,4096]{2,1,0:T(8,128)(2,1)}), bf16[16,16,4096]{2,1,0:T(8,128)(2,1)}, u32[]{:S(2)}, u32[]{:S(2)}) async-start(bf16[16,16,4096]{2,1,0:T(8,128)(2,1)} %bitcast.57), calls=%async_computation.1 | async-start | bytes 4194304 | tf_op jit(solution)/shard_map/all_to_all | solution.py:51
  142.4 93.8 %reduce-scatter.2.cloned.1.call-start = ((), (), s32[]{:S(2)}) async-start(), calls=%async_computation.4 | async-start | bytes 1179648 | tf_op jit(solution)/shard_map/reduce_scatter | solution.py:57
  236.3 8.3 %collective-permute-start = (bf16[128,512]{1,0:T(8,128)(2,1)}, bf16[128,512]{1,0:T(8,128)(2,1)S(1)}, u32[]{:S(2)}, u32[]{:S(2)}) collective-permute-start(bf16[128,512]{1,0:T(8,128)(2,1)} %reduce-scatter.2.cloned.1.call-done), channel_id=1, source_target_pairs={{128,0},{256,128},{384,256},{512,384},{640,512},{768,640},{896,768... | collective-permute-start | bytes 393224 | tf_op jit(solution)/shard_map/ppermute | solution.py:12
Sparse Core Ops, SparseCore 0:
  10.0 56.5 all-gather.1
  193.3 42.9 reduce-scatter.1
where the time goes:
time: 252 us
  waiting for transfers between devices  156 us (62%)
  blocking collectives  55.8 us (22%)
  matrix products  16.3 us (6%)
  between operations  13.5 us (5%)
  starting transfers between devices  7.94 us (3%)
    all_gather x1, waiting for transfers between devices, shards(): whole = lax.all_gather(tokens, 'tensor', axis=1, tiled=True)  58.6 us
    all_to_all x1, blocking collectives, shards(): lax.all_to_all(sent, 'expert', split_axis=0, concat_axis=0, tiled=True)  55.8 us
    all_to_all x1, waiting for transfers between devices, shards(): lax.all_to_all(partial_value.astype(jnp.bfloat16), 'expert', split_axis=0...  47.5 us
    reduce_scatter x1, waiting for transfers between devices, shards(): lax.psum_scatter(summed.astype(jnp.bfloat16), 'tensor', scatter_dimension...  43.1 us
    dot_general x1, matrix products, shards(): lax.dot_general(gate_grad, gate_w, contract_last, preferred_element_type=...  6.09 us
    ppermute x1, waiting for transfers between devices, passed_along(): lax.ppermute(value, axis, [(source, source + steps) for source in range(f...  5.84 us
    all_to_all x1, starting transfers between devices, shards(): lax.all_to_all(partial_value.astype(jnp.bfloat16), 'expert', split_axis=0...  5.47 us
  transfers between devices with their start and end apart: 4, of which 4 were waited for; matrix products, arithmetic and copies ran while one was open for 0% of the time, Pallas kernels for 0%

commit v1 on v0

v1 whole, which is shorter than its diff:
```python
import jax
import jax.numpy as jnp
from jax import lax
from jax.experimental import pallas as pl
from jax.experimental.pallas import tpu as pltpu
from jax.sharding import PartitionSpec as P

MESH = pl.DeviceIdType.MESH
EXP_DEV = 8
CAP = 16
ROUND = 8
CHIP = 2 * CAP
NEAR = (0, 1, 7, 2, 6, 3, 5, 4)
PLACE = tuple(NEAR.index(offset) for offset in range(ROUND))
CHUNKS = 4
ROWS = ROUND * CHIP // CHUNKS
LAST_IN_ORDER = ((((1,), (1,)), ((), ())))


def kernel(
    tok_hbm, gate_hbm, up_hbm, grad_hbm, routes_hbm, slots_hbm, mask_hbm,
    out_ref,
    tok, w, grad_t, routes, slots, mask, grad, sent, x_all, pre, g_all, ring, total, keep_own, keep, back,
    local_sem, x_send, x_recv, f_send, f_recv, b_send, b_recv, o_send, o_recv, k_send, k_recv,
):
    s, e, t = lax.axis_index("section"), lax.axis_index("expert"), lax.axis_index("tensor")
    chip, core = lax.div(e, 2), lax.rem(e, 2)
    width = tok.shape[1]
    half = gate_hbm.shape[0]

    def local(src, dst, index):
        copy = pltpu.make_async_copy(src, dst, local_sem.at[index])
        copy.start()
        return copy

    small = [
        local(routes_hbm, routes, 0), local(slots_hbm, slots, 1),
        local(mask_hbm, mask, 2), local(tok_hbm, tok, 3),
    ]
    large = [local(grad_hbm, grad_t, 4)]
    for rel in range(ROUND):
        columns = pl.ds(pl.multiple_of(lax.rem(t + rel, ROUND) * width, width), width)
        large.append(local(gate_hbm.at[:, columns], w.at[rel, pl.ds(0, half)], 5 + 2 * rel))
        large.append(local(up_hbm.at[:, columns], w.at[rel, pl.ds(half, half)], 6 + 2 * rel))

    up_z, down_z = lax.rem(t + 1, ROUND), lax.rem(t + ROUND - 1, ROUND)
    before, after = lax.rem(s + 7, 8), lax.rem(s + 1, 8)
    barrier = pltpu.get_barrier_semaphore()
    greeted = [(s, lax.rem(e + step, 16), t) for step in range(1, 16)]
    greeted += [(s, e, up_z), (s, e, down_z), (before, e, t), (after, e, t)]
    for device in greeted:
        pl.semaphore_signal(barrier, inc=1, device_id=device, device_id_type=MESH)

    for copy in small:
        copy.wait()
    live = (jnp.bitwise_and(routes[...], EXP_DEV - 1) == 0) & (slots[...] < CAP)
    target = jnp.where(live, lax.shift_right_logical(routes[...], 3) * CAP + slots[...], -1)
    positions = lax.broadcasted_iota(jnp.int32, (16 * CAP, tok.shape[0]), 0)
    hits = jnp.zeros(positions.shape, jnp.float32)
    for k in range(target.shape[0]):
        hits = hits + jnp.where(positions == target[k:k + 1, :], 1.0, 0.0)
    sent[...] = jnp.dot(
        hits.astype(jnp.bfloat16), tok[...], preferred_element_type=jnp.float32
    ).astype(jnp.bfloat16)
    x_all[0, pl.ds(pl.multiple_of(core * CAP, CAP), CAP)] = sent[pl.ds(pl.multiple_of(e * CAP, CAP), CAP)]

    pl.semaphore_wait(barrier, len(greeted))

    sends = []

    def ship(src, dst, send_sem, recv_sem, device):
        copy = pltpu.make_async_remote_copy(
            src_ref=src, dst_ref=dst, send_sem=send_sem, recv_sem=recv_sem,
            device_id=device, device_id_type=MESH,
        )
        copy.start()
        sends.append(copy)

    def to_expert(offset, other):
        to = lax.rem(chip + offset, ROUND) * 2 + other
        place = PLACE[(ROUND - offset) % ROUND]
        ship(
            sent.at[pl.ds(pl.multiple_of(to * CAP, CAP), CAP)],
            x_all.at[0, pl.ds(pl.multiple_of(place * CHIP + core * CAP, CAP), CAP)],
            x_send.at[PLACE[offset], other], x_recv.at[place, core], (s, to, t),
        )

    to_expert(0, 1 - core)
    for offset in NEAR[1:]:
        for other in range(2):
            to_expert(offset, other)

    keep_own[...] = jnp.transpose(hits * mask[...].astype(jnp.float32)).astype(jnp.bfloat16)
    ship(keep_own, keep, k_send.at[0], k_recv.at[0], (before, e, t))

    def landed(ref, send_sem, recv_sem):
        pltpu.make_async_remote_copy(
            src_ref=ref, dst_ref=ref, send_sem=send_sem, recv_sem=recv_sem,
            device_id=(s, e, up_z), device_id_type=MESH,
        ).wait_recv()

    def from_experts(place):
        for other in [1 - core] if place == 0 else range(2):
            rows = pl.ds(pl.multiple_of(place * CHIP + other * CAP, CAP), CAP)
            landed(x_all.at[0, rows], x_send.at[place, other], x_recv.at[place, other])

    def rows_of(chunk):
        return pl.ds(chunk * ROWS, ROWS)

    def up_steps(chunk):
        return 4 if chunk % 2 == 0 else 3

    def down_steps(chunk):
        return 7 - up_steps(chunk)

    def forward(chunk, step):
        rows = rows_of(chunk)
        if step < up_steps(chunk):
            ship(
                x_all.at[(ROUND - step) % ROUND, rows], x_all.at[ROUND - 1 - step, rows],
                f_send.at[0, chunk, step], f_recv.at[0, chunk, step], (s, e, up_z),
            )
        if step < down_steps(chunk):
            ship(
                x_all.at[step, rows], x_all.at[step + 1, rows],
                f_send.at[1, chunk, step], f_recv.at[1, chunk, step], (s, e, down_z),
            )

    def arrived(chunk, step):
        rows = rows_of(chunk)
        rels = []
        if step < up_steps(chunk):
            landed(x_all.at[ROUND - 1 - step, rows], f_send.at[0, chunk, step], f_recv.at[0, chunk, step])
            rels.append(ROUND - 1 - step)
        if step < down_steps(chunk):
            landed(x_all.at[step + 1, rows], f_send.at[1, chunk, step], f_recv.at[1, chunk, step])
            rels.append(step + 1)
        return rels

    def product(chunk, rel):
        return lax.dot_general(
            x_all[rel, chunk * ROWS:(chunk + 1) * ROWS], w[rel], LAST_IN_ORDER,
            preferred_element_type=jnp.float32,
        )

    for chunk in range(CHUNKS):
        for place in range(2 * chunk, 2 * chunk + 2):
            from_experts(place)
        forward(chunk, 0)
    for copy in large:
        copy.wait()
    grad[...] = jnp.transpose(grad_t[...].astype(jnp.float32))
    for chunk in range(CHUNKS):
        pre[chunk] = product(chunk, 0)

    def gradients(chunk):
        value = pre[chunk]
        gate, up = value[:, :half], value[:, half:]
        act = jnp.concatenate(
            [
                grad[pl.ds(pl.multiple_of(lax.rem(chip + NEAR[place], ROUND) * CHIP, CHIP), CHIP)]
                for place in range(2 * chunk, 2 * chunk + 2)
            ],
            axis=0,
        )
        sig = jax.nn.sigmoid(gate)
        up_grad = act * gate * sig
        gate_grad = act * up * sig * (1.0 + gate * (1.0 - sig))
        g_all[chunk] = jnp.concatenate([gate_grad, up_grad], axis=1).astype(jnp.bfloat16)

    def term(chunk, rel):
        return jnp.dot(g_all[chunk], w[rel % ROUND], preferred_element_type=jnp.float32)

    def add_and_send(chunk, direction, hops):
        steps = up_steps(chunk) if direction == 0 else down_steps(chunk)
        if hops > steps:
            return
        value = term(chunk, hops if direction == 0 else ROUND - hops)
        if hops < steps:
            landed(ring.at[direction, chunk, hops], b_send.at[direction, chunk, hops], b_recv.at[direction, chunk, hops])
            value = value + ring[direction, chunk, hops].astype(jnp.float32)
        ring[direction, chunk, hops] = value.astype(jnp.bfloat16)
        ship(
            ring.at[direction, chunk, hops], ring.at[direction, chunk, hops - 1],
            b_send.at[direction, chunk, hops - 1], b_recv.at[direction, chunk, hops - 1],
            (s, e, up_z if direction == 0 else down_z),
        )

    for step in range(4):
        for chunk in range(CHUNKS):
            rels = arrived(chunk, step)
            if step < 3:
                forward(chunk, step + 1)
            value = pre[chunk]
            for rel in rels:
                value = value + product(chunk, rel)
            pre[chunk] = value
            if step == 3:
                gradients(chunk)
                for hops in (4, 3):
                    for direction in range(2):
                        if hops == (up_steps(chunk), down_steps(chunk))[direction]:
                            add_and_send(chunk, direction, hops)

    order = (1, 2, 3, 0)
    for hops in (3, 2, 1):
        for chunk in order:
            for direction in range(2):
                if hops < (up_steps(chunk), down_steps(chunk))[direction]:
                    add_and_send(chunk, direction, hops)
    for chunk in order:
        value = term(chunk, 0)
        for direction in range(2):
            landed(ring.at[direction, chunk, 0], b_send.at[direction, chunk, 0], b_recv.at[direction, chunk, 0])
            value = value + ring[direction, chunk, 0].astype(jnp.float32)
        total[chunk] = value.astype(jnp.bfloat16)
        for place in range(2 * chunk, 2 * chunk + 2):
            for other in range(2):
                to = lax.rem(chip + NEAR[place], ROUND) * 2 + other
                ship(
                    total.at[chunk, pl.ds((place - 2 * chunk) * CHIP + other * CAP, CAP)],
                    back.at[pl.ds(pl.multiple_of(e * CAP, CAP), CAP)],
                    o_send.at[place, other], o_recv.at[e], (before, to, t),
                )

    landed(keep, k_send.at[0], k_recv.at[0])
    for source in range(16):
        landed(back.at[pl.ds(source * CAP, CAP)], o_send.at[0, 0], o_recv.at[source])
    result = jnp.dot(keep[...], back[...], preferred_element_type=jnp.float32)
    out_ref[...] = jnp.where(s == 7, 0.0, result).astype(out_ref.dtype)
    for copy in sends:
        copy.wait_send()


def shards(tokens, w_gate, w_up, hidden_grad, routes, slots, pad_mask):
    rows, width = tokens.shape
    features, half = w_gate.shape[2:]
    slot_rows = hidden_grad.shape[2]
    anywhere = pl.BlockSpec(memory_space=pl.ANY)
    dma = pltpu.SemaphoreType.DMA
    return pl.pallas_call(
        kernel,
        out_shape=jax.ShapeDtypeStruct(tokens.shape, tokens.dtype),
        in_specs=[anywhere] * 7,
        out_specs=pl.BlockSpec(memory_space=pltpu.VMEM),
        scratch_shapes=[
            pltpu.VMEM((rows, width), jnp.bfloat16),
            pltpu.VMEM((ROUND, 2 * half, width), jnp.bfloat16),
            pltpu.VMEM((half, slot_rows), jnp.bfloat16),
            pltpu.VMEM((routes.shape[1], rows), jnp.int32),
            pltpu.VMEM((routes.shape[1], rows), jnp.int32),
            pltpu.VMEM((1, rows), jnp.int32),
            pltpu.VMEM((slot_rows, half), jnp.float32),
            pltpu.VMEM((slot_rows, width), jnp.bfloat16),
            pltpu.VMEM((ROUND, slot_rows, width), jnp.bfloat16),
            pltpu.VMEM((CHUNKS, ROWS, 2 * half), jnp.float32),
            pltpu.VMEM((CHUNKS, ROWS, 2 * half), jnp.bfloat16),
            pltpu.VMEM((2, CHUNKS, 5, ROWS, width), jnp.bfloat16),
            pltpu.VMEM((CHUNKS, ROWS, width), jnp.bfloat16),
            pltpu.VMEM((rows, slot_rows), jnp.bfloat16),
            pltpu.VMEM((rows, slot_rows), jnp.bfloat16),
            pltpu.VMEM((slot_rows, width), jnp.bfloat16),
            dma((5 + 2 * ROUND,)),
            dma((ROUND, 2)),
            dma((ROUND, 2)),
            dma((2, CHUNKS, 4)),
            dma((2, CHUNKS, 4)),
            dma((2, CHUNKS, 4)),
            dma((2, CHUNKS, 4)),
            dma((ROUND, 2)),
            dma((16,)),
            dma((1,)),
            dma((1,)),
        ],
        compiler_params=pltpu.CompilerParams(
            collective_id=0, has_side_effects=True, vmem_limit_bytes=63 * 1024 * 1024
        ),
        cost_estimate=pl.CostEstimate(
            flops=8 * slot_rows * features * half, bytes_accessed=4 * features * half, transcendentals=0
        ),
    )(
        tokens, jnp.swapaxes(w_gate[0, 0], 0, 1), jnp.swapaxes(w_up[0, 0], 0, 1),
        jnp.swapaxes(hidden_grad[0, 0], 0, 1), jnp.swapaxes(routes, 0, 1), jnp.swapaxes(slots, 0, 1),
        pad_mask.reshape(1, rows),
    )


def solution(mesh):
    placed = (
        P(("section", "expert"), "tensor"),
        P("section", "expert", None, "tensor"),
        P("section", "expert", None, "tensor"),
        P("section", "expert", None, "tensor"),
        P(("section", "expert"), None),
        P(("section", "expert"), None),
        P(("section", "expert")),
    )
    return jax.shard_map(
        shards,
        mesh=mesh,
        in_specs=placed,
        out_specs=P(("section", "expert"), "tensor"),
        check_vma=False,
    )
```

time: 252 us -> 83 us (0.33)
  the two profiles are of different devices: /device:TPU:52 before, /device:TPU:51 now
where the time goes in v1:
time: 83 us; the launch traced here: 82.9 us
  Pallas kernels  81.3 us (98%)
  local copies, waits for them, and re-layouts  1.57 us (2%)
    pallas_call x1, Pallas kernels, shards(): pl.pallas_call(kernel, out_shape=jax.ShapeDtypeStruct(tokens.shape, token...  81.3 us

profile of v1, /device:TPU:51, one launch (start us, length us, event | category | flops | bytes accessed | tf_op | source)
XLA Modules:
  0.0 82.9 jit_solution(312186081615903607)
XLA Ops:
  0.0 81.3 %shard_map.73 = bf16[128,512]{1,0:T(8,128)(2,1)} custom-call(bf16[128,512]{1,0:T(8,128)(2,1)} %tok_hbm.1, bf16[192,4096]{1,0:T(8,128)(2,1)} %bitcast.12, bf16[192,4096]{1,0:T(8,128)(2,1)} %bitcast.13, bf16[192,256]{1,0:T(8,128)(2,1)} %bitcast.14, s32[8,128]{1,0:T(8,128)} %bitcast.15, s32[8,128]{1,0:T(8,128)} %bitcast.16, s32[1,128]{1,0:T(1,128)} %bitcast.17), custom_call_target="tpu_custom_call" | custom-call | flops 1610612736 | bytes 3145728 | tf_op jit(solution)/shard_map/pallas_call | solution.py:241
  81.3 1.6 %copy.9 = bf16[128,512]{1,0:T(8,128)(2,1)} copy(bf16[128,512]{1,0:T(8,128)(2,1)} %shard_map.73) | data formatting | bytes 262144

commit v2 on v1

--- a/solution.py
+++ b/solution.py
@@ -13,7 +13,19 @@
 NEAR = (0, 1, 7, 2, 6, 3, 5, 4)
 PLACE = tuple(NEAR.index(offset) for offset in range(ROUND))
 CHUNKS = 4
-ROWS = ROUND * CHIP // CHUNKS
+ORDER = (
+    (0, 0, 1, 0), (0, 0, 0, 0), (0, 1, 1, 0), (0, 1, 0, 0), (0, 2, 0, 0), (0, 2, 1, 0), (1, 0, 0, 0), (0, 3, 1, 0),
+    (1, 0, 1, 0), (0, 3, 0, 0), (1, 2, 1, 0), (1, 2, 0, 0), (1, 3, 1, 0), (1, 1, 1, 0), (1, 0, 0, 1), (1, 3, 0, 0),
+    (1, 2, 1, 1), (1, 2, 0, 1), (1, 3, 1, 1), (1, 0, 0, 2), (1, 1, 0, 0), (1, 1, 1, 1), (1, 0, 1, 1), (1, 3, 0, 1),
+    (1, 2, 1, 2), (1, 3, 1, 2), (1, 2, 0, 2), (1, 0, 0, 3), (1, 1, 1, 2), (1, 1, 0, 1), (1, 0, 1, 2), (2, 0, 0, 4),
+    (2, 0, 1, 3), (1, 3, 0, 2), (1, 3, 1, 3), (2, 3, 0, 3), (2, 3, 1, 4), (1, 2, 0, 3), (2, 2, 1, 3), (2, 2, 0, 4),
+    (1, 1, 1, 3), (1, 1, 0, 2), (2, 1, 1, 4), (2, 1, 0, 3), (2, 3, 1, 3), (2, 0, 1, 2), (2, 3, 0, 2), (2, 2, 0, 3),
+    (2, 1, 1, 3), (2, 1, 0, 2), (2, 3, 1, 2), (2, 2, 1, 2), (2, 0, 0, 3), (2, 2, 0, 2), (2, 1, 1, 2), (2, 3, 0, 1),
+    (2, 3, 1, 1), (2, 0, 0, 2), (2, 2, 1, 1), (2, 2, 0, 1), (2, 1, 0, 1), (2, 1, 1, 1), (3, 3, 0, 0), (2, 0, 0, 1),
+    (2, 0, 1, 1), (3, 2, 0, 0), (3, 1, 0, 0), (3, 0, 0, 0),
+)
+PER = ROUND // CHUNKS
+ROWS = PER * CHIP
 LAST_IN_ORDER = ((((1,), (1,)), ((), ())))
 
 
@@ -21,7 +33,7 @@
     tok_hbm, gate_hbm, up_hbm, grad_hbm, routes_hbm, slots_hbm, mask_hbm,
     out_ref,
     tok, w, grad_t, routes, slots, mask, grad, sent, x_all, pre, g_all, ring, total, keep_own, keep, back,
-    local_sem, x_send, x_recv, f_send, f_recv, b_send, b_recv, o_send, o_recv, k_send, k_recv,
+    local_sem, x_send, x_recv, f_send, f_recv, b_send, b_recv, o_send, o_recv, k_send, k_recv, ready,
 ):
     s, e, t = lax.axis_index("section"), lax.axis_index("expert"), lax.axis_index("tensor")
     chip, core = lax.div(e, 2), lax.rem(e, 2)
@@ -47,9 +59,17 @@
     before, after = lax.rem(s + 7, 8), lax.rem(s + 1, 8)
     barrier = pltpu.get_barrier_semaphore()
     greeted = [(s, lax.rem(e + step, 16), t) for step in range(1, 16)]
-    greeted += [(s, e, up_z), (s, e, down_z), (before, e, t), (after, e, t)]
+    greeted += [(before, e, t), (after, e, t)]
     for device in greeted:
         pl.semaphore_signal(barrier, inc=1, device_id=device, device_id_type=MESH)
+
+    @pl.when(t < ROUND - 1)
+    def _():
+        pl.semaphore_signal(barrier, inc=1, device_id=(s, e, up_z), device_id_type=MESH)
+
+    @pl.when(t == 0)
+    def _():
+        pl.semaphore_signal(barrier, inc=1, device_id=(s, e, down_z), device_id_type=MESH)
 
     for copy in small:
         copy.wait()
@@ -64,26 +84,37 @@
     ).astype(jnp.bfloat16)
     x_all[0, pl.ds(pl.multiple_of(core * CAP, CAP), CAP)] = sent[pl.ds(pl.multiple_of(e * CAP, CAP), CAP)]
 
-    pl.semaphore_wait(barrier, len(greeted))
-
-    sends = []
-
-    def ship(src, dst, send_sem, recv_sem, device):
-        copy = pltpu.make_async_remote_copy(
-            src_ref=src, dst_ref=dst, send_sem=send_sem, recv_sem=recv_sem,
-            device_id=device, device_id_type=MESH,
-        )
-        copy.start()
-        sends.append(copy)
+    pl.semaphore_wait(barrier, len(greeted) + (t + ROUND - 1) // ROUND + t // (ROUND - 1))
+
+    @pl.when(t > 0)
+    def _():
+        pl.semaphore_signal(ready.at[0], inc=1, device_id=(s, e, down_z), device_id_type=MESH)
+
+    @pl.when(t == ROUND - 1)
+    def _():
+        pl.semaphore_signal(ready.at[1], inc=1, device_id=(s, e, up_z), device_id_type=MESH)
+
+    sends = {}
+
+    def ship(operands, *name):
+        def copy():
+            src, dst, send_sem, recv_sem, device = operands()
+            return pltpu.make_async_remote_copy(
+                src_ref=src, dst_ref=dst, send_sem=send_sem, recv_sem=recv_sem,
+                device_id=device, device_id_type=MESH,
+            )
+
+        copy().start()
+        sends[name] = copy
 
     def to_expert(offset, other):
         to = lax.rem(chip + offset, ROUND) * 2 + other
         place = PLACE[(ROUND - offset) % ROUND]
-        ship(
+        ship(lambda: (
             sent.at[pl.ds(pl.multiple_of(to * CAP, CAP), CAP)],
             x_all.at[0, pl.ds(pl.multiple_of(place * CHIP + core * CAP, CAP), CAP)],
-            x_send.at[PLACE[offset], other], x_recv.at[place, core], (s, to, t),
-        )
+            x_send.at[PLACE[offset], other], x_recv.at[place, core], (s, to, t)
+        ), "x", offset, 0 if offset == 0 else other)
 
     to_expert(0, 1 - core)
     for offset in NEAR[1:]:
@@ -91,7 +122,7 @@
             to_expert(offset, other)
 
     keep_own[...] = jnp.transpose(hits * mask[...].astype(jnp.float32)).astype(jnp.bfloat16)
-    ship(keep_own, keep, k_send.at[0], k_recv.at[0], (before, e, t))
+    ship(lambda: (keep_own, keep, k_send.at[0], k_recv.at[0], (before, e, t)), "k")
 
     def landed(ref, send_sem, recv_sem):
         pltpu.make_async_remote_copy(
@@ -104,6 +135,9 @@
             rows = pl.ds(pl.multiple_of(place * CHIP + other * CAP, CAP), CAP)
             landed(x_all.at[0, rows], x_send.at[place, other], x_recv.at[place, other])
 
+    def places(chunk):
+        return range(PER * chunk, PER * (chunk + 1))
+
     def rows_of(chunk):
         return pl.ds(chunk * ROWS, ROWS)
 
@@ -113,26 +147,26 @@
     def down_steps(chunk):
         return 7 - up_steps(chunk)
 
-    def forward(chunk, step):
+    def forward(chunk, step, directions=(0, 1)):
         rows = rows_of(chunk)
-        if step < up_steps(chunk):
-            ship(
+        if step < up_steps(chunk) and 0 in directions:
+            ship(lambda: (
                 x_all.at[(ROUND - step) % ROUND, rows], x_all.at[ROUND - 1 - step, rows],
-                f_send.at[0, chunk, step], f_recv.at[0, chunk, step], (s, e, up_z),
-            )
-        if step < down_steps(chunk):
-            ship(
+                f_send.at[0, chunk, step], f_recv.at[0, chunk, step], (s, e, up_z)
+            ), "f", 0, chunk, step)
+        if step < down_steps(chunk) and 1 in directions:
+            ship(lambda: (
                 x_all.at[step, rows], x_all.at[step + 1, rows],
-                f_send.at[1, chunk, step], f_recv.at[1, chunk, step], (s, e, down_z),
-            )
-
-    def arrived(chunk, step):
+                f_send.at[1, chunk, step], f_recv.at[1, chunk, step], (s, e, down_z)
+            ), "f", 1, chunk, step)
+
+    def arrived(chunk, step, directions=(0, 1)):
         rows = rows_of(chunk)
         rels = []
-        if step < up_steps(chunk):
+        if step < up_steps(chunk) and 0 in directions:
             landed(x_all.at[ROUND - 1 - step, rows], f_send.at[0, chunk, step], f_recv.at[0, chunk, step])
             rels.append(ROUND - 1 - step)
-        if step < down_steps(chunk):
+        if step < down_steps(chunk) and 1 in directions:
             landed(x_all.at[step + 1, rows], f_send.at[1, chunk, step], f_recv.at[1, chunk, step])
             rels.append(step + 1)
         return rels
@@ -142,16 +176,6 @@
             x_all[rel, chunk * ROWS:(chunk + 1) * ROWS], w[rel], LAST_IN_ORDER,
             preferred_element_type=jnp.float32,
         )
-
-    for chunk in range(CHUNKS):
-        for place in range(2 * chunk, 2 * chunk + 2):
-            from_experts(place)
-        forward(chunk, 0)
-    for copy in large:
-        copy.wait()
-    grad[...] = jnp.transpose(grad_t[...].astype(jnp.float32))
-    for chunk in range(CHUNKS):
-        pre[chunk] = product(chunk, 0)
 
     def gradients(chunk):
         value = pre[chunk]
@@ -159,7 +183,7 @@
         act = jnp.concatenate(
             [
                 grad[pl.ds(pl.multiple_of(lax.rem(chip + NEAR[place], ROUND) * CHIP, CHIP), CHIP)]
-                for place in range(2 * chunk, 2 * chunk + 2)
+                for place in places(chunk)
             ],
             axis=0,
         )
@@ -180,56 +204,79 @@
             landed(ring.at[direction, chunk, hops], b_send.at[direction, chunk, hops], b_recv.at[direction, chunk, hops])
             value = value + ring[direction, chunk, hops].astype(jnp.float32)
         ring[direction, chunk, hops] = value.astype(jnp.bfloat16)
-        ship(
+        ship(lambda: (
             ring.at[direction, chunk, hops], ring.at[direction, chunk, hops - 1],
             b_send.at[direction, chunk, hops - 1], b_recv.at[direction, chunk, hops - 1],
-            (s, e, up_z if direction == 0 else down_z),
-        )
-
-    for step in range(4):
-        for chunk in range(CHUNKS):
-            rels = arrived(chunk, step)
-            if step < 3:
-                forward(chunk, step + 1)
-            value = pre[chunk]
-            for rel in rels:
-                value = value + product(chunk, rel)
-            pre[chunk] = value
-            if step == 3:
-                gradients(chunk)
-                for hops in (4, 3):
-                    for direction in range(2):
-                        if hops == (up_steps(chunk), down_steps(chunk))[direction]:
-                            add_and_send(chunk, direction, hops)
-
-    order = (1, 2, 3, 0)
-    for hops in (3, 2, 1):
-        for chunk in order:
-            for direction in range(2):
-                if hops < (up_steps(chunk), down_steps(chunk))[direction]:
-                    add_and_send(chunk, direction, hops)
-    for chunk in order:
+            (s, e, up_z if direction == 0 else down_z)
+        ), "b", direction, chunk, hops)
+
+    def to_tokens(place, other):
+        to = lax.rem(chip + NEAR[place], ROUND) * 2 + other
+        ship(lambda: (
+            total.at[place // PER, pl.ds(place % PER * CHIP + other * CAP, CAP)],
+            back.at[pl.ds(pl.multiple_of(e * CAP, CAP), CAP)],
+            o_send.at[place, other], o_recv.at[e], (before, to, t)
+        ), "o", place, other)
+
+    def own(chunk, direction, _):
+        if chunk not in begun:
+            for place in places(chunk):
+                from_experts(place)
+            begun.add(chunk)
+        if direction not in met:
+            met.add(direction)
+
+            @pl.when(t < ROUND - 1 if direction == 0 else t == 0)
+            def _():
+                pl.semaphore_wait(ready.at[direction], 1)
+
+        forward(chunk, 0, (direction,))
+        if direction == 0:
+            take(chunk, 0)
+
+    def pass_on(chunk, direction, step):
+        (rel,) = arrived(chunk, step, (direction,))
+        forward(chunk, step + 1, (direction,))
+        take(chunk, rel)
+
+    def take(chunk, rel):
+        if not filled:
+            for copy in large:
+                copy.wait()
+            grad[...] = jnp.transpose(grad_t[...].astype(jnp.float32))
+        if chunk in filled:
+            pre[chunk] += product(chunk, rel)
+        else:
+            pre[chunk] = product(chunk, rel)
+        filled.add(chunk)
+
+    def add(chunk, direction, hops):
+        if chunk not in turned:
+            gradients(chunk)
+            turned.add(chunk)
+        add_and_send(chunk, direction, hops)
+
+    def finish(chunk, *_):
         value = term(chunk, 0)
         for direction in range(2):
             landed(ring.at[direction, chunk, 0], b_send.at[direction, chunk, 0], b_recv.at[direction, chunk, 0])
             value = value + ring[direction, chunk, 0].astype(jnp.float32)
         total[chunk] = value.astype(jnp.bfloat16)
-        for place in range(2 * chunk, 2 * chunk + 2):
+        for place in places(chunk):
             for other in range(2):
-                to = lax.rem(chip + NEAR[place], ROUND) * 2 + other
-                ship(
-                    total.at[chunk, pl.ds((place - 2 * chunk) * CHIP + other * CAP, CAP)],
-                    back.at[pl.ds(pl.multiple_of(e * CAP, CAP), CAP)],
-                    o_send.at[place, other], o_recv.at[e], (before, to, t),
-                )
+                to_tokens(place, other)
+
+    begun, met, filled, turned = set(), set(), set(), set()
+    for kind, chunk, direction, step in ORDER:
+        (own, pass_on, add, finish)[kind](chunk, direction, step)
 
     landed(keep, k_send.at[0], k_recv.at[0])
     for source in range(16):
         landed(back.at[pl.ds(source * CAP, CAP)], o_send.at[0, 0], o_recv.at[source])
     result = jnp.dot(keep[...], back[...], preferred_element_type=jnp.float32)
     out_ref[...] = jnp.where(s == 7, 0.0, result).astype(out_ref.dtype)
-    for copy in sends:
-        copy.wait_send()
+    for copy in sends.values():
+        copy().wait_send()
 
 
 def shards(tokens, w_gate, w_up, hidden_grad, routes, slots, pad_mask):
@@ -271,6 +318,7 @@
             dma((16,)),
             dma((1,)),
             dma((1,)),
+            pltpu.SemaphoreType.REGULAR((2,)),
         ],
         compiler_params=pltpu.CompilerParams(
             collective_id=0, has_side_effects=True, vmem_limit_bytes=63 * 1024 * 1024

time: 83 us -> 78.3 us (0.943)
  the two profiles are of different devices: /device:TPU:51 before, /device:TPU:49 now
where the time goes in v2:
time: 78.3 us; the launch traced here: 78.1 us
  Pallas kernels  76.6 us (98%)
  local copies, waits for them, and re-layouts  1.57 us (2%)
    pallas_call x1, Pallas kernels, shards(): pl.pallas_call(kernel, out_shape=jax.ShapeDtypeStruct(tokens.shape, token...  76.6 us
    unnamed x1, local copies, waits for them, and re-layouts  1.57 us

profile of v2, /device:TPU:49, one launch (start us, length us, event | category | flops | bytes accessed | tf_op | source)
XLA Modules:
  0.0 78.1 jit_solution(3386436123663912646)
XLA Ops:
  0.0 76.6 %shard_map.73 = bf16[128,512]{1,0:T(8,128)(2,1)} custom-call(bf16[128,512]{1,0:T(8,128)(2,1)} %tok_hbm.1, bf16[192,4096]{1,0:T(8,128)(2,1)} %bitcast.12, bf16[192,4096]{1,0:T(8,128)(2,1)} %bitcast.13, bf16[192,256]{1,0:T(8,128)(2,1)} %bitcast.14, s32[8,128]{1,0:T(8,128)} %bitcast.15, s32[8,128]{1,0:T(8,128)} %bitcast.16, s32[1,128]{1,0:T(1,128)} %bitcast.17), custom_call_target="tpu_custom_call" | custom-call | flops 1610612736 | bytes 3145728 | tf_op jit(solution)/shard_map/pallas_call | solution.py:288
  76.6 1.6 %copy.9 = bf16[128,512]{1,0:T(8,128)(2,1)} copy(bf16[128,512]{1,0:T(8,128)(2,1)} %shard_map.73) | data formatting | bytes 262144

commit v3 on v2

--- a/solution.py
+++ b/solution.py
@@ -24,6 +24,7 @@
     (2, 3, 1, 1), (2, 0, 0, 2), (2, 2, 1, 1), (2, 2, 0, 1), (2, 1, 0, 1), (2, 1, 1, 1), (3, 3, 0, 0), (2, 0, 0, 1),
     (2, 0, 1, 1), (3, 2, 0, 0), (3, 1, 0, 0), (3, 0, 0, 0),
 )
+IN_FLIGHT = 3
 PER = ROUND // CHUNKS
 ROWS = PER * CHIP
 LAST_IN_ORDER = ((((1,), (1,)), ((), ())))
@@ -31,8 +32,8 @@
 
 def kernel(
     tok_hbm, gate_hbm, up_hbm, grad_hbm, routes_hbm, slots_hbm, mask_hbm,
-    out_ref,
-    tok, w, grad_t, routes, slots, mask, grad, sent, x_all, pre, g_all, ring, total, keep_own, keep, back,
+    keep, back,
+    tok, w, grad_t, routes, slots, mask, grad, sent, x_all, pre, g_all, ring, total, keep_own,
     local_sem, x_send, x_recv, f_send, f_recv, b_send, b_recv, o_send, o_recv, k_send, k_recv, ready,
 ):
     s, e, t = lax.axis_index("section"), lax.axis_index("expert"), lax.axis_index("tensor")
@@ -94,7 +95,7 @@
     def _():
         pl.semaphore_signal(ready.at[1], inc=1, device_id=(s, e, up_z), device_id_type=MESH)
 
-    sends = {}
+    sends, queues = {}, ([], [])
 
     def ship(operands, *name):
         def copy():
@@ -104,6 +105,11 @@
                 device_id=device, device_id_type=MESH,
             )
 
+        if name[0] in ("f", "b"):
+            queue = queues[name[1]]
+            queue.append(name)
+            if len(queue) > IN_FLIGHT:
+                sends.pop(queue.pop(0))().wait_send()
         copy().start()
         sends[name] = copy
 
@@ -270,12 +276,14 @@
     for kind, chunk, direction, step in ORDER:
         (own, pass_on, add, finish)[kind](chunk, direction, step)
 
+    last = [copy for name, copy in sends.items() if name[0] == "o"]
+    for name, copy in sends.items():
+        if name[0] != "o":
+            copy().wait_send()
     landed(keep, k_send.at[0], k_recv.at[0])
     for source in range(16):
         landed(back.at[pl.ds(source * CAP, CAP)], o_send.at[0, 0], o_recv.at[source])
-    result = jnp.dot(keep[...], back[...], preferred_element_type=jnp.float32)
-    out_ref[...] = jnp.where(s == 7, 0.0, result).astype(out_ref.dtype)
-    for copy in sends.values():
+    for copy in last:
         copy().wait_send()
 
 
@@ -285,11 +293,14 @@
     slot_rows = hidden_grad.shape[2]
     anywhere = pl.BlockSpec(memory_space=pl.ANY)
     dma = pltpu.SemaphoreType.DMA
-    return pl.pallas_call(
+    keep, back = pl.pallas_call(
         kernel,
-        out_shape=jax.ShapeDtypeStruct(tokens.shape, tokens.dtype),
+        out_shape=[
+            jax.ShapeDtypeStruct((rows, slot_rows), jnp.bfloat16),
+            jax.ShapeDtypeStruct((slot_rows, width), jnp.bfloat16),
+        ],
         in_specs=[anywhere] * 7,
-        out_specs=pl.BlockSpec(memory_space=pltpu.VMEM),
+        out_specs=[anywhere] * 2,
         scratch_shapes=[
             pltpu.VMEM((rows, width), jnp.bfloat16),
             pltpu.VMEM((ROUND, 2 * half, width), jnp.bfloat16),
@@ -305,8 +316,6 @@
             pltpu.VMEM((2, CHUNKS, 5, ROWS, width), jnp.bfloat16),
             pltpu.VMEM((CHUNKS, ROWS, width), jnp.bfloat16),
             pltpu.VMEM((rows, slot_rows), jnp.bfloat16),
-            pltpu.VMEM((rows, slot_rows), jnp.bfloat16),
-            pltpu.VMEM((slot_rows, width), jnp.bfloat16),
             dma((5 + 2 * ROUND,)),
             dma((ROUND, 2)),
             dma((ROUND, 2)),
@@ -331,6 +340,8 @@
         jnp.swapaxes(hidden_grad[0, 0], 0, 1), jnp.swapaxes(routes, 0, 1), jnp.swapaxes(slots, 0, 1),
         pad_mask.reshape(1, rows),
     )
+    result = jnp.dot(keep, back, preferred_element_type=jnp.float32)
+    return jnp.where(lax.axis_index("section") == 7, 0.0, result).astype(tokens.dtype)
 
 
 def solution(mesh):

time: 78.3 us -> 77.7 us (level)
  matrix products: 0 us -> 1.84 us
  local copies, waits for them, and re-layouts: 1.57 us -> 0 us
  Pallas kernels: 76.6 us -> 75.7 us
    dot_general x0 -> x1, matrix products: none -> 1.84 us  [shards(): result = jnp.dot(keep, back, preferred_element_type=jnp.float32)]
    unnamed x1 -> x0, local copies, waits for them, and re-layouts: 1.57 us -> none
    pallas_call x1, Pallas kernels: 76.6 us -> 75.7 us  [shards(): pl.pallas_call(kernel, out_shape=[jax.ShapeDtypeStruct((rows, slot_rows),...]
where the time goes in v3:
time: 77.7 us; the launch traced here: 77.6 us
  Pallas kernels  75.7 us (97%)
  matrix products  1.84 us (2%)
    pallas_call x1, Pallas kernels, shards(): pl.pallas_call(kernel, out_shape=[jax.ShapeDtypeStruct((rows, slot_rows),...  75.7 us
    dot_general x1, matrix products, shards(): result = jnp.dot(keep, back, preferred_element_type=jnp.float32)  1.84 us

profile of v3, /device:TPU:49, one launch (start us, length us, event | category | flops | bytes accessed | tf_op | source)
XLA Modules:
  0.0 77.6 jit_solution(14459096796979952631)
XLA Ops:
  0.0 75.7 %shard_map.73 = (bf16[128,256]{1,0:T(8,128)(2,1)}, bf16[256,512]{1,0:T(8,128)(2,1)}) custom-call(bf16[128,512]{1,0:T(8,128)(2,1)} %tok_hbm.1, bf16[192,4096]{1,0:T(8,128)(2,1)} %bitcast.14, bf16[192,4096]{1,0:T(8,128)(2,1)} %bitcast.15, bf16[192,256]{1,0:T(8,128)(2,1)} %bitcast.16, s32[8,128]{1,0:T(8,128)} %bitcast.17, s32[8,128]{1,0:T(8,128)} %bitcast.18, ...), custom_call_target="tpu_custom_call" | custom-call | flops 1610612736 | bytes 3145728 | tf_op jit(solution)/shard_map/pallas_call | solution.py:296
  75.7 1.8 %fusion = bf16[128,512]{1,0:T(8,128)(2,1)} fusion(bf16[128,256]{1,0:T(8,128)(2,1)} %get-tuple-element.7, bf16[256,512]{1,0:T(8,128)(2,1)} %get-tuple-element.8, pred[]{:T(512)S(6)} %eq.3), kind=kOutput, calls=%fused_computation.1 | convolution fusion | flops 33685504 | bytes 458753 | tf_op jit(solution)/shard_map/dot_general | solution.py:343
